TPU v7x, 512 devices: a whole 4x4x16 slice. The times are simulated.
512 devices in a mesh: pair: 128 (over y, z, core), red: 4 (over x).
Axes of the slice: x: 4, y: 4, z: 16, core: 2. Of those that a mesh axis runs over, the one named last changes fastest.
Arguments:
- amplitudes: bfloat16 [2048, 4096], P('pair', 'red'), may hold values from -6 to 6
- integrals: bfloat16 [4096, 65536], P('red', 'pair'), may hold values from -0.125 to 0.125
- pattern: int32 [128, 64], P('pair', 'red'), may hold values from 0 to 1, as said below
Outputs:
- ladder_term: bfloat16 [128, 16, 65536], P(None, 'red', 'pair')
Inputs may be any that keep to these rules, and one draw needn't show every extreme that they name: `pattern`: in every tile, exactly 8 of each aligned group of 16 blocks are 1.
All inputs are finite; a program needn't handle non-finite values.
Results may differ from a plain program's by a relative error of at most 0.0013.
Values may be sent and summed in bfloat16 or wider, within the bound.
A program may use at most 64 MiB of HBM per device.

v0:
```python
import jax
import jax.numpy as jnp
from jax import lax
from jax.sharding import PartitionSpec as P


def shards(amplitudes, integrals, pattern):
    tile_rows = amplitudes.shape[0]
    blocks = pattern.shape[1]
    block_width = amplitudes.shape[1] // blocks
    out_width = integrals.shape[1]
    keep_mask = jnp.repeat(jnp.repeat(pattern, tile_rows, axis=0), block_width, axis=1).astype(
        jnp.bfloat16
    )
    masked = amplitudes * keep_mask
    partial_value = jnp.dot(
        lax.all_gather(masked, "pair", axis=0, tiled=True),
        integrals,
        preferred_element_type=jnp.float32,
    )
    tile_count = partial_value.shape[0] // tile_rows
    summed = lax.psum_scatter(
        partial_value.reshape(tile_count, tile_rows, out_width),
        "red",
        scatter_dimension=1,
        tiled=True,
    )
    return summed.astype(jnp.bfloat16)


def solution(mesh):
    placed = (P("pair", "red"), P("red", "pair"), P("pair", "red"))
    return jax.shard_map(
        shards, mesh=mesh, in_specs=placed, out_specs=P(None, "red", "pair"), check_vma=False
    )
```

profile of v0, /device:TPU:1, one launch (start us, length us, event | category | flops | bytes accessed | tf_op | source)
XLA Modules:
  0.0 226.7 jit_solution(17842721416136384331)
XLA Ops:
  6.5 0.0 copy-start
  6.5 0.0 all-gather.2.cloned.1.call-start
  6.5 0.7 convert_bitcast_fusion
  7.3 0.1 broadcast_in_dim.6
  7.4 0.1 convert_element_type.16
  7.4 1.4 broadcast_multiply_fusion
  8.8 0.0 all-gather.2.cloned.1.call-update
  8.9 0.0 reduce-scatter.2.cloned.1.call-start
  8.9 149.4 %all-gather.2.cloned.1.call-done = bf16[2048,1024]{1,0:T(8,128)(2,1)} async-done(((bf16[16,1024]{1,0:T(8,128)(2,1)}), bf16[2048,1024]{1,0:T(8,128)(2,1)}) %all-gather.2.cloned.1.call-update) | async-done | bytes 4194320 | tf_op jit(solution)/shard_map/all_gather | solution.py:17
  158.3 0.0 copy-done
  158.3 4.5 %fusion = f32[2048,512]{1,0:T(8,128)S(1)} fusion(bf16[2048,1024]{1,0:T(8,128)(2,1)} %all-gather.2.cloned.1.call-done, bf16[1024,512]{1,0:T(8,128)(2,1)S(1)} %copy-done), kind=kOutput, calls=%fused_computation.2 | convolution fusion | flops 2147483648 | bytes 9437184 | tf_op jit(solution)/shard_map/dot_general | solution.py:16
  162.8 4.4 %copy.4 = f32[128,16,512]{2,0,1:T(8,128)} copy(f32[128,16,512]{2,1,0:T(8,128)S(1)} %bitcast.5) | data formatting | bytes 8388608 | tf_op jit(solution)/shard_map/reshape | solution.py:23
  167.2 0.0 reduce-scatter.2.cloned.1.call-update
  167.2 50.2 %reduce-scatter.2.cloned.1.call-done = f32[128,4,512]{2,0,1:T(8,128)} async-done(((f32[128,16,512]{2,0,1:T(8,128)}), f32[128,4,512]{2,0,1:T(8,128)}) %reduce-scatter.2.cloned.1.call-update) | async-done | bytes 1048592 | tf_op jit(solution)/shard_map/reduce_scatter | solution.py:22
  217.3 1.3 convert_element_type.17
  218.6 1.2 copy.5
Async XLA Ops:
  6.5 151.7 %copy-start = (bf16[1024,512]{1,0:T(8,128)(2,1)S(1)}, bf16[1024,512]{1,0:T(8,128)(2,1)}, u32[]{:S(2)}) copy-start(bf16[1024,512]{1,0:T(8,128)(2,1)} %param.4) | copy-start | bytes 3145732
  6.5 151.7 %all-gather.2.cloned.1.call-start = ((), (), s32[]{:S(2)}) async-start(), calls=%async_computation.1 | async-start | bytes 4227072 | tf_op jit(solution)/shard_map/all_gather | solution.py:17
  8.9 208.5 %reduce-scatter.2.cloned.1.call-start = ((), (), s32[]{:S(2)}) async-start(), calls=%async_computation.2 | async-start | bytes 5242880 | tf_op jit(solution)/shard_map/reduce_scatter | solution.py:22
Sparse Core Ops, SparseCore 0:
  10.5 147.7 all-gather.1
  167.3 49.9 reduce-scatter.1
where the time goes:
time: 227 us
  waiting for transfers between devices  200 us (88%)
  between operations  13.4 us (6%)
  local copies, waits for them, and re-layouts  5.73 us (3%)
  matrix products  4.53 us (2%)
  other arithmetic  3.41 us (2%)
    all_gather x1, waiting for transfers between devices, shards(): lax.all_gather(masked, 'pair', axis=0, tiled=True)  149 us
    reduce_scatter x1, waiting for transfers between devices, shards(): lax.psum_scatter(partial_value.reshape(tile_count, tile_rows, out_width),...  50.2 us
  transfers between devices with their start and end apart: 2, of which 2 were waited for; matrix products, arithmetic and copies ran while one was open for 0% of the time, Pallas kernels for 0%

commit v1 on v0

v1 whole, which is shorter than its diff:
```python
import functools

import jax
import jax.numpy as jnp
from jax import lax
from jax.experimental import pallas as pl
from jax.experimental.pallas import tpu as pltpu
from jax.sharding import PartitionSpec as P

MESH = pl.DeviceIdType.MESH
NY, NZ, NX = 4, 16, 4
OFFSETS = (0, 1, -1, 2, -2, 3, -3, 4, -4, 5, -5, 6, -6, 7, -7, 8)
SLOT = {off % NZ: slot for slot, off in enumerate(OFFSETS)}
BATCHES = ((0, 1), (1, 5), (5, 9), (9, 13), (13, 16))
ROWS = 16
BW = 64
BLOCKS = 16
KEPT = 8
LEVELS = 32760.0


def both_halves(pair):
    low = lax.broadcasted_iota(jnp.int32, pair.shape, 1) < BW
    turned = pltpu.roll(pair, BW, 1)
    return jnp.where(low, pair, turned), jnp.where(low, turned, pair)


def kernel(
    amp_ref, pat_ref, int_ref, out_ref,
    tiles, dense, sums, b_ref, xs, xr, ss, sr,
    b_sem, zs_sem, zr_sem, ys_sem, yr_sem, cs_sem, cr_sem, xs_sem, xr_sem, ss_sem, sr_sem,
):
    pair, r = lax.axis_index("pair"), lax.axis_index("red")
    y, z, c = pair // (2 * NZ), (pair // 2) % NZ, pair % 2

    def at_y(d):
        return (((y + d) % NY) * (2 * NZ) + z * 2 + c, r)

    def at_z(d):
        return (y * (2 * NZ) + ((z + d) % NZ) * 2 + c, r)

    def at_x(d):
        return (pair, (r + d) % NX)

    sibling = (pair + 1 - 2 * c, r)

    load_b = pltpu.make_async_copy(int_ref, b_ref, b_sem)
    load_b.start()

    barrier = pltpu.get_barrier_semaphore()
    peers = [at_z(d) for d in OFFSETS[1:]] + [at_y(d) for d in range(1, NY)]
    peers += [at_x(d) for d in range(1, NX)] + [sibling]
    for peer in peers:
        pl.semaphore_signal(barrier, inc=1, device_id=peer, device_id_type=MESH)

    half = lax.broadcasted_iota(jnp.int32, (ROWS, 2 * BW), 1) // BW
    row = lax.broadcasted_iota(jnp.int32, (ROWS, 2 * BW), 0)
    place, seen = [], jnp.int32(0)
    for b in range(BLOCKS):
        keep = pat_ref[0, b] > 0
        place.append(jnp.where(keep, seen, 99))
        seen = seen + jnp.where(keep, 1, 0)
    blocks = []
    for j in range(BLOCKS // 2):
        blocks += both_halves(amp_ref[:, 2 * BW * j : 2 * BW * (j + 1)].astype(jnp.float32))
    code = jnp.zeros((ROWS, 2 * BW), jnp.int32)
    for b in range(BLOCKS):
        code = jnp.where((row == b // 2) & (half == b % 2), place[b], code)
    for j in range(KEPT // 2):
        acc = jnp.zeros((ROWS, 2 * BW), jnp.float32)
        for b in range(2 * j, min(BLOCKS, 2 * j + 10)):
            acc = jnp.where(half + 2 * j == place[b], blocks[b], acc)
        tiles[y, c, 0, :, 2 * BW * j : 2 * BW * (j + 1)] = acc.astype(jnp.bfloat16)
    tiles[y, c, 0, :, KEPT * BW :] = code.astype(jnp.float32).astype(jnp.bfloat16)

    pl.semaphore_wait(barrier, len(peers))

    def remote(src, dst, send, recv, device):
        return pltpu.make_async_remote_copy(
            src_ref=src, dst_ref=dst, send_sem=send, recv_sem=recv,
            device_id=device, device_id_type=MESH,
        )

    def z_copy(d):
        slot = SLOT[-d % NZ]
        return remote(
            tiles.at[y, c, 0], tiles.at[y, c, slot], zs_sem.at[slot], zr_sem.at[slot], at_z(d)
        )

    def y_copy(d, k):
        a, b = BATCHES[k]
        part = tiles.at[y, c, a:b]
        return remote(part, part, ys_sem.at[d - 1, k], yr_sem.at[d - 1, k], at_y(d))

    def core_copy(d, k):
        a, b = BATCHES[k]
        part = tiles.at[(y - d + NY) % NY, c, a:b]
        return remote(part, part, cs_sem.at[d, k], cr_sem.at[d, k], sibling)

    def x_copies(d, k):
        a, b = BATCHES[k]
        rows = slice(32 * a, 32 * b)
        return (
            remote(ss.at[d - 1, k], sr.at[d - 1, k], ss_sem.at[d - 1, k], sr_sem.at[d - 1, k], at_x(d)),
            remote(xs.at[d - 1, rows], xr.at[d - 1, rows], xs_sem.at[d - 1, k], xr_sem.at[d - 1, k], at_x(d)),
        )

    def from_z(k):
        a, b = BATCHES[k]
        if k:
            for slot in range(a, b):
                z_copy(-OFFSETS[slot]).wait_recv()
        for d in range(1, NY):
            y_copy(d, k).start()
        core_copy(0, k).start()

    def from_y(k):
        for d in range(1, NY):
            y_copy(d, k).wait_recv()
            core_copy(d, k).start()

    def unpack(k):
        a, b = BATCHES[k]
        n = b - a

        def one(i, _):
            yy, cc, s = i // (2 * n), (i // n) % 2, i % n
            places = tiles[yy, cc, a + s, :, KEPT * BW :].astype(jnp.float32)
            kept = []
            for j in range(KEPT // 2):
                kept += both_halves(
                    tiles[yy, cc, a + s, :, 2 * BW * j : 2 * BW * (j + 1)].astype(jnp.float32)
                )
            for j in range(BLOCKS // 2):
                wanted = jnp.broadcast_to(places[j : j + 1, :], (ROWS, 2 * BW))
                acc = jnp.zeros((ROWS, 2 * BW), jnp.float32)
                for q in range(max(0, 2 * j - 8), min(KEPT, 2 * j + 2)):
                    acc = jnp.where(wanted == float(q), kept[q], acc)
                dense[yy, cc, s, :, 2 * BW * j : 2 * BW * (j + 1)] = acc.astype(jnp.bfloat16)
            return 0

        lax.fori_loop(0, 8 * n, one, 0)

    def multiply(k):
        a, b = BATCHES[k]
        n = b - a

        def one(i, _):
            ys = pl.ds(2 * i, 2)
            lhs = dense[ys, :, 0:n].reshape(4 * n * ROWS, BLOCKS * BW)
            prod = jnp.dot(lhs, b_ref[...], preferred_element_type=jnp.float32)
            prod = prod.reshape(2, 2, n, 2, 8, prod.shape[-1])
            first, second = prod[:, 0], prod[:, 1]
            upper = lax.broadcasted_iota(jnp.int32, first.shape, 3) < 4
            even = jnp.where(upper, first, pltpu.roll(second, 4, 3))
            odd = jnp.where(upper, pltpu.roll(first, 4, 3), second)
            for h in range(2):
                sums[2 * h, ys, a:b] = even[:, :, h]
                sums[2 * h + 1, ys, a:b] = odd[:, :, h]
            return 0

        lax.fori_loop(0, 2, one, 0)

    def compute(k):
        a, b = BATCHES[k]
        n = b - a
        for d in range(NY):
            other = tiles.at[(y - d + NY) % NY, 1 - c, a:b]
            remote(other, other, cs_sem.at[d, k], cr_sem.at[d, k], sibling).wait_recv()
        unpack(k)
        if k == 0:
            load_b.wait()
        multiply(k)
        for d in (2, 1, 3):
            values = sums[(r + d) % NX, :, a:b].reshape(32 * n, sums.shape[-1])
            top = jnp.maximum(jnp.max(jnp.abs(values), axis=0, keepdims=True), 1e-30)
            scaled = jnp.round(values * (LEVELS / top))
            xs[d - 1, 32 * a : 32 * b] = scaled.astype(jnp.int32).astype(jnp.int16)
            ss[d - 1, k] = top * (1.0 / LEVELS)
            for copy in x_copies(d, k):
                copy.start()

    def finish(k):
        a, b = BATCHES[k]
        n = b - a
        total = sums[r, :, a:b].reshape(32 * n, sums.shape[-1])
        for d in (1, 3, 2):
            for copy in x_copies(d, k):
                copy.wait_recv()
            part = xr[d - 1, 32 * a : 32 * b].astype(jnp.int32).astype(jnp.float32)
            total = total + part * sr[d - 1, k]
        total = total.astype(jnp.bfloat16).reshape(NY, n, 8, total.shape[-1])
        for s in range(n):
            out_ref[:, (z + OFFSETS[a + s] + NZ) % NZ] = total[:, s]

    for off in OFFSETS[1:]:
        z_copy(off).start()
    from_z(0)
    from_y(0)
    from_z(1)
    compute(0)
    from_y(1)
    from_z(2)
    compute(1)
    from_y(2)
    from_z(3)
    compute(2)
    finish(0)
    from_y(3)
    from_z(4)
    compute(3)
    finish(1)
    from_y(4)
    compute(4)
    finish(2)
    finish(3)
    finish(4)
    for off in OFFSETS[1:]:
        z_copy(off).wait_send()
    for k in range(len(BATCHES)):
        for d in range(1, NY):
            y_copy(d, k).wait_send()
        for d in range(NY):
            core_copy(d, k).wait_send()
        for d in range(1, NX):
            for copy in x_copies(d, k):
                copy.wait_send()


def shards(amplitudes, integrals, pattern):
    depth, width = integrals.shape
    count = len(BATCHES)
    dma = pltpu.SemaphoreType.DMA
    out = pl.pallas_call(
        kernel,
        out_shape=jax.ShapeDtypeStruct((NY, NZ, 8, width), jnp.bfloat16),
        in_specs=[
            pl.BlockSpec(memory_space=pltpu.VMEM),
            pl.BlockSpec(memory_space=pltpu.SMEM),
            pl.BlockSpec(memory_space=pl.ANY),
        ],
        out_specs=pl.BlockSpec(memory_space=pltpu.VMEM),
        scratch_shapes=[
            pltpu.VMEM((NY, 2, NZ, ROWS, (KEPT + 2) * BW), jnp.bfloat16),
            pltpu.VMEM((NY, 2, 4, ROWS, depth), jnp.bfloat16),
            pltpu.VMEM((NX, NY, NZ, 8, width), jnp.float32),
            pltpu.VMEM((depth, width), jnp.bfloat16),
            pltpu.VMEM((NX - 1, 32 * NZ, width), jnp.int16),
            pltpu.VMEM((NX - 1, 32 * NZ, width), jnp.int16),
            pltpu.VMEM((NX - 1, count, 1, width), jnp.float32),
            pltpu.VMEM((NX - 1, count, 1, width), jnp.float32),
            dma(()),
            dma((NZ,)),
            dma((NZ,)),
            dma((NY - 1, count)),
            dma((NY - 1, count)),
            dma((NY, count)),
            dma((NY, count)),
            dma((NX - 1, count)),
            dma((NX - 1, count)),
            dma((NX - 1, count)),
            dma((NX - 1, count)),
        ],
        compiler_params=pltpu.CompilerParams(
            collective_id=0, has_side_effects=True, vmem_limit_bytes=48 * 2**20
        ),
    )(amplitudes, pattern, integrals)
    return out.reshape(NY * NZ * 2, 4, width)


def solution(mesh):
    placed = (P("pair", "red"), P("red", "pair"), P("pair", "red"))
    return jax.shard_map(
        shards, mesh=mesh, in_specs=placed, out_specs=P(None, "red", "pair"), check_vma=False
    )
```

time: 227 us -> 66.2 us (0.29)
  waiting for transfers between devices: 200 us -> 0 us
  Pallas kernels: 0 us -> 62.4 us
  between operations: 13.4 us -> 0.01 us
  matrix products: 4.53 us -> 0 us
  other arithmetic: 3.41 us -> 0 us
    all_gather x1 -> x0, waiting for transfers between devices: 149 us -> none  [shards(): lax.all_gather(masked, 'pair', axis=0, tiled=True)]
    pallas_call x0 -> x1, Pallas kernels: none -> 62.4 us  [shards(): pl.pallas_call(kernel, out_shape=jax.ShapeDtypeStruct((NY, NZ, 8, width),...]
    reduce_scatter x1 -> x0, waiting for transfers between devices: 50.2 us -> none  [shards(): lax.psum_scatter(partial_value.reshape(tile_count, tile_rows, out_width),...]
    dot_general x1 -> x0, matrix products: 4.53 us -> none  [shards(): jnp.dot(lax.all_gather(masked, 'pair', axis=0, tiled=True), integrals, pr...]
    reshape x1, local copies, waits for them, and re-layouts: 4.37 us -> 0.92 us  [shards(): return out.reshape(NY * NZ * 2, 4, width)]
    unnamed x2 -> x6, local copies, waits for them, and re-layouts: 0.01 us -> 2.64 us
  transfers between devices with their start and end apart: 2 -> 0, of which waited for: 2 -> 0; matrix products, arithmetic and copies ran while one was open for 0% -> 0% of each run, Pallas kernels for 0% -> 0%
where the time goes in v1:
time: 66.2 us; the launch traced here: 66 us
  Pallas kernels  62.4 us (94%)
  local copies, waits for them, and re-layouts  3.55 us (5%)
    pallas_call x1, Pallas kernels, shards(): pl.pallas_call(kernel, out_shape=jax.ShapeDtypeStruct((NY, NZ, 8, width),...  62.4 us
    unnamed x6, local copies, waits for them, and re-layouts  2.64 us

profile of v1, /device:TPU:1, one launch (start us, length us, event | category | flops | bytes accessed | tf_op | source)
XLA Modules:
  0.0 66.0 jit_solution(18179071031634928547)
XLA Ops:
  0.0 0.0 copy-start
  0.0 1.2 %copy-done = bf16[1024,512]{1,0:T(8,128)(2,1)S(1)} copy-done((bf16[1024,512]{1,0:T(8,128)(2,1)S(1)}, bf16[1024,512]{1,0:T(8,128)(2,1)}, u32[]{:S(2)}) %copy-start) | copy-done | bytes 1048600
  1.2 0.0 copy-start.1
  1.2 0.8 %copy-done.1 = bf16[16,1024]{1,0:T(8,128)(2,1)S(1)} copy-done((bf16[16,1024]{1,0:T(8,128)(2,1)S(1)}, bf16[16,1024]{1,0:T(8,128)(2,1)}, u32[]{:S(2)}) %copy-start.1) | copy-done | bytes 32792
  2.0 0.0 copy-start.2
  2.0 0.7 copy-done.2
  2.6 62.4 %shard_map.37 = bf16[4,16,8,512]{3,2,1,0:T(8,128)(2,1)S(1)} custom-call(bf16[16,1024]{1,0:T(8,128)(2,1)S(1)} %copy-done.1, s32[1,16]{1,0:T(1,128)S(1)} %copy-done.2, bf16[1024,512]{1,0:T(8,128)(2,1)S(1)} %copy-done), custom_call_target="tpu_custom_call" | custom-call | tf_op jit(solution)/shard_map/pallas_call | solution.py:234
  65.1 0.9 %reshape.3 = bf16[128,4,512]{2,1,0:T(4,128)(2,1)} reshape(bf16[4,16,8,512]{3,2,1,0:T(8,128)(2,1)S(1)} %shard_map.37) | data formatting | bytes 1048576 | tf_op jit(solution)/shard_map/reshape | solution.py:268
Async XLA Ops:
  0.0 1.2 %copy-start = (bf16[1024,512]{1,0:T(8,128)(2,1)S(1)}, bf16[1024,512]{1,0:T(8,128)(2,1)}, u32[]{:S(2)}) copy-start(bf16[1024,512]{1,0:T(8,128)(2,1)} %int_ref.1) | copy-start | bytes 3145732
  1.2 0.8 %copy-start.1 = (bf16[16,1024]{1,0:T(8,128)(2,1)S(1)}, bf16[16,1024]{1,0:T(8,128)(2,1)}, u32[]{:S(2)}) copy-start(bf16[16,1024]{1,0:T(8,128)(2,1)} %amp_ref.1) | copy-start | bytes 98308
  2.0 0.7 copy-start.2

commit v2 on v1

v2 whole, which is shorter than its diff:
```python
import jax
import jax.numpy as jnp
from jax import lax
from jax.experimental import pallas as pl
from jax.experimental.pallas import tpu as pltpu
from jax.sharding import PartitionSpec as P

MESH = pl.DeviceIdType.MESH
NY, NZ, NX = 4, 16, 4
OFFSETS = (0, 4, -4, 1, -1, 2, -2, 3, -3, 5, -5, 6, -6, 7, -7, 8)
REACH = 4
SLOT = {off % NZ: slot for slot, off in enumerate(OFFSETS)}
BATCHES = ((0, 1), (1, 5), (5, 9), (9, 13), (13, 16))
ROWS = 16
BW = 64
LANES = 2 * BW
BLOCKS = 16
KEPT = 8
DATA = KEPT * BW
PARTS = 4


def both_halves(pair):
    low = lax.broadcasted_iota(jnp.int32, pair.shape, 1) < BW
    turned = pltpu.roll(pair, BW, 1)
    return jnp.where(low, pair, turned), jnp.where(low, turned, pair)


def turn(arrays):
    upper = lax.broadcasted_iota(jnp.int32, (8, LANES), 0) < 4
    out = []
    for b in range(4):
        part = [v[8 * (b // 2) : 8 * (b // 2) + 8] for v in arrays]
        if b % 2 == 0:
            halves = [jnp.where(upper, part[i], pltpu.roll(part[i + 1], 4, 0)) for i in (0, 2)]
        else:
            halves = [jnp.where(upper, pltpu.roll(part[i], 4, 0), part[i + 1]) for i in (0, 2)]
        out.append(jnp.concatenate(halves, axis=0))
    return out


def kernel(
    amp_ref, pat_ref, int_ref, out_ref,
    pieces, given, tiles, spread, lhs, slices, total,
    b_sem, xs_sem, xr_sem, zs_sem, zr_sem, ys_sem, yr_sem, cs_sem, cr_sem, bs_sem, br_sem,
):
    pair, r = lax.axis_index("pair"), lax.axis_index("red")
    y, z, c = pair // (2 * NZ), (pair // 2) % NZ, pair % 2
    depth, width = int_ref.shape

    def at_y(d):
        return (((y + d) % NY) * (2 * NZ) + z * 2 + c, r)

    def at_z(d):
        return (y * (2 * NZ) + ((z + d) % NZ) * 2 + c, r)

    def at_x(d):
        return (pair, (r + d) % NX)

    sibling = (pair + 1 - 2 * c, r)

    load_b = pltpu.make_async_copy(int_ref, slices.at[r], b_sem)
    load_b.start()

    barrier = pltpu.get_barrier_semaphore()
    near = OFFSETS[1 : 1 + 2 * REACH]
    peers = [at_z(d) for d in near] + [at_y(d) for d in range(1, NY)]
    peers += [at_x(d) for d in range(1, NX)] + [sibling]
    for peer in peers:
        pl.semaphore_signal(barrier, inc=1, device_id=peer, device_id_type=MESH)

    def remote(src, dst, send, recv, device):
        return pltpu.make_async_remote_copy(
            src_ref=src, dst_ref=dst, send_sem=send, recv_sem=recv,
            device_id=device, device_id_type=MESH,
        )

    lane = lax.broadcasted_iota(jnp.int32, (ROWS, LANES), 1)
    row = lax.broadcasted_iota(jnp.int32, (ROWS, LANES), 0)
    place, seen = [], jnp.int32(0)
    for b in range(BLOCKS):
        keep = pat_ref[0, b] > 0
        place.append(jnp.where(keep, seen, 99))
        seen = seen + jnp.where(keep, 1, 0)
    blocks = []
    for j in range(BLOCKS // 2):
        blocks += both_halves(amp_ref[:, LANES * j : LANES * (j + 1)].astype(jnp.float32))
    code = jnp.zeros((ROWS, LANES), jnp.int32)
    for b in range(BLOCKS):
        code = jnp.where(lane == b, place[b], code)
    code = code.astype(jnp.float32).astype(jnp.bfloat16)
    packed = []
    for j in range(KEPT // 2):
        acc = jnp.zeros((ROWS, LANES), jnp.float32)
        for b in range(2 * j, min(BLOCKS, 2 * j + 10)):
            acc = jnp.where(lane // BW + 2 * j == place[b], blocks[b], acc)
        packed.append(acc)
    for d, piece in enumerate(turn(packed)):
        pieces[d, :, :LANES] = piece.astype(jnp.bfloat16)
        pieces[d, :, LANES:] = code
    given[r] = pieces[r]
    wide = lax.broadcasted_iota(jnp.int32, spread.shape, 1) // BW
    spread[...] = jnp.where(
        lax.broadcasted_iota(jnp.int32, spread.shape, 0) == wide, 1.0, 0.0
    ).astype(jnp.bfloat16)

    pl.semaphore_wait(barrier, len(peers))

    def x_copy(d):
        return remote(
            pieces.at[(r + d) % NX], given.at[r], xs_sem.at[d - 1], xr_sem.at[d - 1], at_x(d)
        )

    def z_copy(d):
        slot = SLOT[-d % NZ]
        if abs(d) <= REACH:
            held, device = 0, at_z(d)
        elif abs(d) < 2 * REACH:
            on = REACH if d > 0 else -REACH
            held, device = SLOT[-on % NZ], at_z(d - on)
        else:
            held = jnp.where(c == 0, SLOT[-REACH % NZ], SLOT[REACH])
            device = at_z(REACH - 2 * REACH * c + NZ)
        return remote(
            tiles.at[y, c, held], tiles.at[y, c, slot], zs_sem.at[slot], zr_sem.at[slot], device
        )

    def y_copy(d, k):
        a, b = BATCHES[k]
        part = tiles.at[y, c, a:b]
        return remote(part, part, ys_sem.at[d - 1, k], yr_sem.at[d - 1, k], at_y(d))

    def core_copy(d, k, own=True):
        a, b = BATCHES[k]
        part = tiles.at[(y - d + NY) % NY, c if own else 1 - c, a:b]
        return remote(part, part, cs_sem.at[d, k], cr_sem.at[d, k], sibling)

    rows = depth // PARTS
    half = PARTS // 2

    def own_slice(side, i):
        part = slice(rows * i, rows * (i + 1))
        return remote(
            int_ref.at[part], slices.at[r, part], bs_sem.at[side, i], br_sem.at[side, i], at_x(1 + 2 * side)
        )

    def next_slice(side, i):
        first = rows * (i + half * side)
        part = slices.at[(r + 3 - 2 * side) % NX, first : first + rows]
        return remote(
            part, part, bs_sem.at[side, PARTS + i], br_sem.at[side, PARTS + i], at_x(1 + 2 * side)
        )

    def arrival(side, i):
        if i < PARTS:
            owner, first = (r + 3 - 2 * side) % NX, rows * i
        else:
            owner, first = (r + 2) % NX, rows * (i - PARTS + half * side)
        part = slices.at[owner, first : first + rows]
        return remote(part, part, bs_sem.at[side, i], br_sem.at[side, i], at_x(1 + 2 * side))

    def from_z(k):
        a, b = BATCHES[k]
        if k:
            for slot in range(a, b):
                z_copy(-OFFSETS[slot]).wait_recv()
                if abs(OFFSETS[slot]) == REACH:
                    for more in range(3, 0, -1):
                        z_copy(-OFFSETS[slot] // REACH * (REACH + more)).start()
            if k == 1:
                z_copy(2 * REACH).start()
        for d in range(1, NY):
            y_copy(d, k).start()
        core_copy(0, k).start()

    def from_y(k):
        for d in range(1, NY):
            y_copy(d, k).wait_recv()
            core_copy(d, k).start()

    def send_on(i):
        for side in range(2):
            arrival(side, i + half * side).wait_recv()
            next_slice(side, i).start()

    def unpack(k):
        a, b = BATCHES[k]
        for d in range(NY):
            core_copy(d, k, own=False).wait_recv()

        def one(i, _):
            slot, first = a + i // 2, 2 * (i % 2)
            four = [(first + t // 2, t % 2) for t in range(4)]
            places = jnp.concatenate([tiles[yy, cc, slot, :, DATA:] for yy, cc in four], axis=0)
            wanted = jnp.dot(places, spread[...], preferred_element_type=jnp.float32)
            kept = []
            for yy, cc in four:
                have = []
                for j in range(KEPT // 2):
                    have += both_halves(
                        tiles[yy, cc, slot, :, LANES * j : LANES * (j + 1)].astype(jnp.float32)
                    )
                kept.append(have)
            for j in range(BLOCKS // 2):
                full = []
                for t in range(4):
                    want = wanted[ROWS * t : ROWS * (t + 1), LANES * j : LANES * (j + 1)]
                    acc = jnp.zeros((ROWS, LANES), jnp.float32)
                    for q in range(max(0, 2 * j - 8), min(KEPT, 2 * j + 2)):
                        acc = jnp.where(want == float(q), kept[t][q], acc)
                    full.append(acc)
                for s, piece in enumerate(turn(full)):
                    lhs[s, 2 * a + i, :, LANES * j : LANES * (j + 1)] = piece.astype(jnp.bfloat16)
            return 0

        lax.fori_loop(0, 2 * (b - a), one, 0)

    def multiply(a, b, distances, add):
        def one(i, _):
            columns = pl.ds(pl.multiple_of(i * (width // 2), width // 2), width // 2)
            value = total[32 * a : 32 * b, columns] if add else None
            for d in distances:
                s = (r + d) % NX
                left = lhs[s, 2 * a : 2 * b].reshape(32 * (b - a), depth)
                term = jnp.dot(left, slices[s, :, columns], preferred_element_type=jnp.float32)
                value = term if value is None else value + term
            total[32 * a : 32 * b, columns] = value
            return 0

        lax.fori_loop(0, 2, one, 0)

    for d in (2, 1, 3):
        x_copy(d).start()
    for i in range(PARTS):
        own_slice(0, i).start()
        own_slice(1, (i + half) % PARTS).start()
    for d in range(1, NX):
        came = given.at[(r - d + NX) % NX]
        remote(came, came, xs_sem.at[d - 1], xr_sem.at[d - 1], at_x(d)).wait_recv()
    whole = turn([given[s, :, :LANES].astype(jnp.float32) for s in range(NX)])
    for j in range(KEPT // 2):
        tiles[y, c, 0, :, LANES * j : LANES * (j + 1)] = whole[j].astype(jnp.bfloat16)
    code = jnp.zeros((ROWS, LANES), jnp.float32)
    for s in range(NX):
        code = jnp.where(row // 4 == s, given[s, :, LANES:].astype(jnp.float32), code)
    tiles[y, c, 0, :, DATA:] = code.astype(jnp.bfloat16)

    for off in near:
        z_copy(off).start()
    from_z(0)
    from_z(1)
    from_z(2)
    from_z(3)
    from_z(4)
    send_on(0)
    from_y(0)
    from_y(1)
    unpack(0)
    from_y(2)
    unpack(1)
    from_y(3)
    send_on(1)
    from_y(4)
    unpack(2)
    unpack(3)
    load_b.wait()
    for i in range(PARTS):
        for side in range(2):
            if i // half != side:
                arrival(side, i).wait_recv()
    most = BATCHES[3][1]
    multiply(0, most, (0, 1, 3), False)
    unpack(4)
    multiply(most, NZ, (0, 1, 3), False)
    for i in range(half):
        for side in range(2):
            arrival(side, PARTS + i).wait_recv()
    multiply(0, NZ, (2,), True)
    for slot, off in enumerate(OFFSETS):
        result = total[32 * slot : 32 * (slot + 1)].astype(jnp.bfloat16)
        out_ref[:, (z + off + NZ) % NZ] = result.reshape(NY, 8, width)

    for d in range(1, NX):
        x_copy(d).wait_send()
    for off in OFFSETS[1:]:
        z_copy(off).wait_send()
    for k in range(len(BATCHES)):
        for d in range(1, NY):
            y_copy(d, k).wait_send()
        for d in range(NY):
            core_copy(d, k).wait_send()
    for side in range(2):
        for i in range(PARTS):
            own_slice(side, i).wait_send()
        for i in range(half):
            next_slice(side, i).wait_send()


def shards(amplitudes, integrals, pattern):
    depth, width = integrals.shape
    count = len(BATCHES)
    dma = pltpu.SemaphoreType.DMA
    out = pl.pallas_call(
        kernel,
        out_shape=jax.ShapeDtypeStruct((NY, NZ, 8, width), jnp.bfloat16),
        in_specs=[
            pl.BlockSpec(memory_space=pltpu.VMEM),
            pl.BlockSpec(memory_space=pltpu.SMEM),
            pl.BlockSpec(memory_space=pltpu.HBM),
        ],
        out_specs=pl.BlockSpec(memory_space=pltpu.VMEM),
        scratch_shapes=[
            pltpu.VMEM((NX, ROWS, 2 * LANES), jnp.bfloat16),
            pltpu.VMEM((NX, ROWS, 2 * LANES), jnp.bfloat16),
            pltpu.VMEM((NY, 2, NZ, ROWS, DATA + LANES), jnp.bfloat16),
            pltpu.VMEM((LANES, depth), jnp.bfloat16),
            pltpu.VMEM((NX, 2 * NZ, ROWS, depth), jnp.bfloat16),
            pltpu.VMEM((NX, depth, width), jnp.bfloat16),
            pltpu.VMEM((32 * NZ, width), jnp.float32),
            dma(()),
            dma((NX - 1,)),
            dma((NX - 1,)),
            dma((NZ,)),
            dma((NZ,)),
            dma((NY - 1, count)),
            dma((NY - 1, count)),
            dma((NY, count)),
            dma((NY, count)),
            dma((2, PARTS + PARTS // 2)),
            dma((2, PARTS + PARTS // 2)),
        ],
        compiler_params=pltpu.CompilerParams(
            collective_id=0, has_side_effects=True, vmem_limit_bytes=62 * 2**20
        ),
    )(amplitudes, pattern, integrals)
    return out.reshape(NY * NZ * 2, 4, width)


def solution(mesh):
    placed = (P("pair", "red"), P("red", "pair"), P("pair", "red"))
    return jax.shard_map(
        shards, mesh=mesh, in_specs=placed, out_specs=P(None, "red", "pair"), check_vma=False
    )
```

time: 66.2 us -> 55.1 us (0.83)
  Pallas kernels: 62.4 us -> 52.9 us
  local copies, waits for them, and re-layouts: 3.55 us -> 1.96 us
    pallas_call x1, Pallas kernels: 62.4 us -> 52.9 us  [shards(): pl.pallas_call(kernel, out_shape=jax.ShapeDtypeStruct((NY, NZ, 8, width),...]
    unnamed x6 -> x0, local copies, waits for them, and re-layouts: 2.64 us -> none
    reshape x1, local copies, waits for them, and re-layouts: 0.92 us -> 1.96 us  [shards(): return out.reshape(NY * NZ * 2, 4, width)]
where the time goes in v2:
time: 55.1 us; the launch traced here: 54.8 us
  Pallas kernels  52.9 us (96%)
  local copies, waits for them, and re-layouts  1.96 us (4%)
    pallas_call x1, Pallas kernels, shards(): pl.pallas_call(kernel, out_shape=jax.ShapeDtypeStruct((NY, NZ, 8, width),...  52.9 us
    reshape x1, local copies, waits for them, and re-layouts, shards(): return out.reshape(NY * NZ * 2, 4, width)  1.96 us

profile of v2, /device:TPU:1, one launch (start us, length us, event | category | flops | bytes accessed | tf_op | source)
XLA Modules:
  0.0 54.8 jit_solution(3682156909444743483)
XLA Ops:
  0.0 52.9 %shard_map.37 = bf16[4,16,8,512]{3,2,1,0:T(8,128)(2,1)} custom-call(bf16[16,1024]{1,0:T(8,128)(2,1)} %amp_ref.1, s32[1,16]{1,0:T(1,128)} %pat_ref.1, bf16[1024,512]{1,0:T(8,128)(2,1)} %int_ref.1), custom_call_target="tpu_custom_call" | custom-call | tf_op jit(solution)/shard_map/pallas_call | solution.py:303
  52.9 2.0 %reshape.3 = bf16[128,4,512]{2,1,0:T(4,128)(2,1)} reshape(bf16[4,16,8,512]{3,2,1,0:T(8,128)(2,1)} %shard_map.37) | data formatting | bytes 1048576 | tf_op jit(solution)/shard_map/reshape | solution.py:336

commit v3 on v2

--- a/solution.py
+++ b/solution.py
@@ -42,7 +42,7 @@
 def kernel(
     amp_ref, pat_ref, int_ref, out_ref,
     pieces, given, tiles, spread, lhs, slices, total,
-    b_sem, xs_sem, xr_sem, zs_sem, zr_sem, ys_sem, yr_sem, cs_sem, cr_sem, bs_sem, br_sem,
+    b_sem, xs_sem, xr_sem, zs_sem, zr_sem, ys_sem, yr_sem, cs_sem, cr_sem, bs_sem, br_sem, hello,
 ):
     pair, r = lax.axis_index("pair"), lax.axis_index("red")
     y, z, c = pair // (2 * NZ), (pair // 2) % NZ, pair % 2
@@ -64,7 +64,7 @@
 
     barrier = pltpu.get_barrier_semaphore()
     near = OFFSETS[1 : 1 + 2 * REACH]
-    peers = [at_z(d) for d in near] + [at_y(d) for d in range(1, NY)]
+    peers = [at_z(-d) for d in range(1, REACH + 1)] + [at_y(d) for d in range(1, NY)]
     peers += [at_x(d) for d in range(1, NX)] + [sibling]
     for peer in peers:
         pl.semaphore_signal(barrier, inc=1, device_id=peer, device_id_type=MESH)
@@ -229,6 +229,8 @@
 
         lax.fori_loop(0, 2, one, 0)
 
+    for d in range(1, REACH + 1):
+        pl.semaphore_signal(hello.at[d - 1], inc=1, device_id=at_z(d), device_id_type=MESH)
     for d in (2, 1, 3):
         x_copy(d).start()
     for i in range(PARTS):
@@ -246,14 +248,18 @@
     tiles[y, c, 0, :, DATA:] = code.astype(jnp.bfloat16)
 
     for off in near:
-        z_copy(off).start()
+        if off > 0:
+            z_copy(off).start()
     from_z(0)
+    from_y(0)
+    for d in (4, 1, 2, 3):
+        pl.semaphore_wait(hello.at[d - 1], 1)
+        z_copy(-d).start()
     from_z(1)
     from_z(2)
     from_z(3)
     from_z(4)
     send_on(0)
-    from_y(0)
     from_y(1)
     unpack(0)
     from_y(2)
@@ -268,7 +274,7 @@
         for side in range(2):
             if i // half != side:
                 arrival(side, i).wait_recv()
-    most = BATCHES[3][1]
+    most = BATCHES[-2][1]
     multiply(0, most, (0, 1, 3), False)
     unpack(4)
     multiply(most, NZ, (0, 1, 3), False)
@@ -278,7 +284,11 @@
     multiply(0, NZ, (2,), True)
     for slot, off in enumerate(OFFSETS):
         result = total[32 * slot : 32 * (slot + 1)].astype(jnp.bfloat16)
-        out_ref[:, (z + off + NZ) % NZ] = result.reshape(NY, 8, width)
+        place_in = 2 * ((z + off + NZ) % NZ)
+        for yy in range(NY):
+            for cc in range(2):
+                first = 8 * yy + 4 * cc
+                out_ref[2 * NZ * yy + cc + place_in] = result[first : first + 4]
 
     for d in range(1, NX):
         x_copy(d).wait_send()
@@ -302,7 +312,7 @@
     dma = pltpu.SemaphoreType.DMA
     out = pl.pallas_call(
         kernel,
-        out_shape=jax.ShapeDtypeStruct((NY, NZ, 8, width), jnp.bfloat16),
+        out_shape=jax.ShapeDtypeStruct((2 * NY * NZ, 4, width), jnp.bfloat16),
         in_specs=[
             pl.BlockSpec(memory_space=pltpu.VMEM),
             pl.BlockSpec(memory_space=pltpu.SMEM),
@@ -328,12 +338,13 @@
             dma((NY, count)),
             dma((2, PARTS + PARTS // 2)),
             dma((2, PARTS + PARTS // 2)),
+            pltpu.SemaphoreType.REGULAR((REACH,)),
         ],
         compiler_params=pltpu.CompilerParams(
             collective_id=0, has_side_effects=True, vmem_limit_bytes=62 * 2**20
         ),
     )(amplitudes, pattern, integrals)
-    return out.reshape(NY * NZ * 2, 4, width)
+    return out
 
 
 def solution(mesh):

time: 55.1 us -> 53.4 us (0.969)
  Pallas kernels: 52.9 us -> 51.2 us
    unnamed x0 -> x1, local copies, waits for them, and re-layouts: none -> 2.02 us
    reshape x1 -> x0, local copies, waits for them, and re-layouts: 1.96 us -> none  [shards(): return out.reshape(NY * NZ * 2, 4, width)]
    pallas_call x1, Pallas kernels: 52.9 us -> 51.2 us  [shards(): pl.pallas_call(kernel, out_shape=jax.ShapeDtypeStruct((2 * NY * NZ, 4, wi...]
where the time goes in v3:
time: 53.4 us; the launch traced here: 53.2 us
  Pallas kernels  51.2 us (96%)
  local copies, waits for them, and re-layouts  2.02 us (4%)
    pallas_call x1, Pallas kernels, shards(): pl.pallas_call(kernel, out_shape=jax.ShapeDtypeStruct((2 * NY * NZ, 4, wi...  51.2 us
    unnamed x1, local copies, waits for them, and re-layouts  2.02 us

profile of v3, /device:TPU:1, one launch (start us, length us, event | category | flops | bytes accessed | tf_op | source)
XLA Modules:
  0.0 53.2 jit_solution(14959597186908370260)
XLA Ops:
  0.0 51.2 %shard_map.37 = bf16[128,4,512]{2,1,0:T(4,128)(2,1)} custom-call(bf16[16,1024]{1,0:T(8,128)(2,1)} %amp_ref.1, s32[1,16]{1,0:T(1,128)} %pat_ref.1, bf16[1024,512]{1,0:T(8,128)(2,1)} %int_ref.1), custom_call_target="tpu_custom_call" | custom-call | tf_op jit(solution)/shard_map/pallas_call | solution.py:313
  51.2 2.0 %copy.5 = bf16[128,4,512]{2,1,0:T(4,128)(2,1)} copy(bf16[128,4,512]{2,1,0:T(4,128)(2,1)} %shard_map.37) | data formatting | bytes 1048576

commit v4 on v3

--- a/solution.py
+++ b/solution.py
@@ -7,9 +7,10 @@
 
 MESH = pl.DeviceIdType.MESH
 NY, NZ, NX = 4, 16, 4
-OFFSETS = (0, 4, -4, 1, -1, 2, -2, 3, -3, 5, -5, 6, -6, 7, -7, 8)
+OFFSETS = (0, 1, -1, 2, -2, 4, -4, 3, -3, 5, -5, 6, -6, 7, -7, 8)
 REACH = 4
 SLOT = {off % NZ: slot for slot, off in enumerate(OFFSETS)}
+PLANE = 1
 BATCHES = ((0, 1), (1, 5), (5, 9), (9, 13), (13, 16))
 ROWS = 16
 BW = 64
@@ -63,8 +64,7 @@
     load_b.start()
 
     barrier = pltpu.get_barrier_semaphore()
-    near = OFFSETS[1 : 1 + 2 * REACH]
-    peers = [at_z(-d) for d in range(1, REACH + 1)] + [at_y(d) for d in range(1, NY)]
+    peers = [at_z(-1), at_z(-2)] + [at_y(d) for d in range(1, NY)]
     peers += [at_x(d) for d in range(1, NX)] + [sibling]
     for peer in peers:
         pl.semaphore_signal(barrier, inc=1, device_id=peer, device_id_type=MESH)
@@ -125,6 +125,17 @@
             tiles.at[y, c, held], tiles.at[y, c, slot], zs_sem.at[slot], zr_sem.at[slot], device
         )
 
+    def plane_copy(d):
+        slot = SLOT[-d % NZ]
+        return remote(
+            tiles.at[:, c, 0], tiles.at[:, c, slot], zs_sem.at[slot], zr_sem.at[slot], at_z(d)
+        )
+
+    def plane_core_copy(own=True):
+        a, b = BATCHES[PLANE]
+        part = tiles.at[:, c if own else 1 - c, a:b]
+        return remote(part, part, cs_sem.at[0, PLANE], cr_sem.at[0, PLANE], sibling)
+
     def y_copy(d, k):
         a, b = BATCHES[k]
         part = tiles.at[y, c, a:b]
@@ -167,14 +178,14 @@
                 if abs(OFFSETS[slot]) == REACH:
                     for more in range(3, 0, -1):
                         z_copy(-OFFSETS[slot] // REACH * (REACH + more)).start()
-            if k == 1:
+            if k == 2:
                 z_copy(2 * REACH).start()
-        for d in range(1, NY):
+        for d in (2, 1, 3):
             y_copy(d, k).start()
         core_copy(0, k).start()
 
     def from_y(k):
-        for d in range(1, NY):
+        for d in (1, 3, 2):
             y_copy(d, k).wait_recv()
             core_copy(d, k).start()
 
@@ -185,14 +196,18 @@
 
     def unpack(k):
         a, b = BATCHES[k]
-        for d in range(NY):
-            core_copy(d, k, own=False).wait_recv()
+        if k == PLANE:
+            plane_core_copy(own=False).wait_recv()
+        else:
+            for d in range(NY):
+                core_copy(d, k, own=False).wait_recv()
 
         def one(i, _):
             slot, first = a + i // 2, 2 * (i % 2)
             four = [(first + t // 2, t % 2) for t in range(4)]
             places = jnp.concatenate([tiles[yy, cc, slot, :, DATA:] for yy, cc in four], axis=0)
             wanted = jnp.dot(places, spread[...], preferred_element_type=jnp.float32)
+            wanted = wanted.astype(jnp.bfloat16)
             kept = []
             for yy, cc in four:
                 have = []
@@ -200,15 +215,15 @@
                     have += both_halves(
                         tiles[yy, cc, slot, :, LANES * j : LANES * (j + 1)].astype(jnp.float32)
                     )
-                kept.append(have)
+                kept.append([block.astype(jnp.bfloat16) for block in have])
             for j in range(BLOCKS // 2):
                 full = []
                 for t in range(4):
                     want = wanted[ROWS * t : ROWS * (t + 1), LANES * j : LANES * (j + 1)]
-                    acc = jnp.zeros((ROWS, LANES), jnp.float32)
+                    acc = jnp.zeros((ROWS, LANES), jnp.bfloat16)
                     for q in range(max(0, 2 * j - 8), min(KEPT, 2 * j + 2)):
-                        acc = jnp.where(want == float(q), kept[t][q], acc)
-                    full.append(acc)
+                        acc = jnp.where(want == jnp.bfloat16(q), kept[t][q], acc)
+                    full.append(acc.astype(jnp.float32))
                 for s, piece in enumerate(turn(full)):
                     lhs[s, 2 * a + i, :, LANES * j : LANES * (j + 1)] = piece.astype(jnp.bfloat16)
             return 0
@@ -229,7 +244,7 @@
 
         lax.fori_loop(0, 2, one, 0)
 
-    for d in range(1, REACH + 1):
+    for d in (1, 2):
         pl.semaphore_signal(hello.at[d - 1], inc=1, device_id=at_z(d), device_id_type=MESH)
     for d in (2, 1, 3):
         x_copy(d).start()
@@ -247,35 +262,42 @@
         code = jnp.where(row // 4 == s, given[s, :, LANES:].astype(jnp.float32), code)
     tiles[y, c, 0, :, DATA:] = code.astype(jnp.bfloat16)
 
-    for off in near:
-        if off > 0:
-            z_copy(off).start()
     from_z(0)
+    pl.semaphore_wait(hello.at[1], 1)
+    pl.semaphore_wait(hello.at[0], 1)
+    pl.semaphore_signal(hello.at[2], inc=1, device_id=at_z(-2), device_id_type=MESH)
+    pl.semaphore_signal(hello.at[3], inc=1, device_id=at_z(2), device_id_type=MESH)
+    pl.semaphore_wait(hello.at[2], 1)
+    z_copy(4).start()
+    pl.semaphore_wait(hello.at[3], 1)
+    for d in (-4, 3, -3):
+        z_copy(d).start()
     from_y(0)
-    for d in (4, 1, 2, 3):
-        pl.semaphore_wait(hello.at[d - 1], 1)
-        z_copy(-d).start()
-    from_z(1)
+    for d in (1, -1, 2, -2):
+        plane_copy(d).start()
     from_z(2)
+    for d in (1, -1, 2, -2):
+        plane_copy(-d).wait_recv()
+    plane_core_copy().start()
     from_z(3)
     from_z(4)
     send_on(0)
-    from_y(1)
+    from_y(2)
     unpack(0)
-    from_y(2)
     unpack(1)
     from_y(3)
     send_on(1)
-    from_y(4)
     unpack(2)
-    unpack(3)
     load_b.wait()
     for i in range(PARTS):
         for side in range(2):
             if i // half != side:
                 arrival(side, i).wait_recv()
-    most = BATCHES[-2][1]
-    multiply(0, most, (0, 1, 3), False)
+    multiply(0, BATCHES[2][1], (0, 1, 3), False)
+    from_y(4)
+    unpack(3)
+    middle, most = BATCHES[2][1], BATCHES[-2][1]
+    multiply(middle, most, (0, 1, 3), False)
     unpack(4)
     multiply(most, NZ, (0, 1, 3), False)
     for i in range(half):
@@ -293,8 +315,14 @@
     for d in range(1, NX):
         x_copy(d).wait_send()
     for off in OFFSETS[1:]:
-        z_copy(off).wait_send()
+        if abs(off) <= 2:
+            plane_copy(off).wait_send()
+        else:
+            z_copy(off).wait_send()
+    plane_core_copy().wait_send()
     for k in range(len(BATCHES)):
+        if k == PLANE:
+            continue
         for d in range(1, NY):
             y_copy(d, k).wait_send()
         for d in range(NY):

time: 53.4 us -> 49.7 us (0.931)
  Pallas kernels: 51.2 us -> 47.5 us
    pallas_call x1, Pallas kernels: 51.2 us -> 47.5 us  [shards(): pl.pallas_call(kernel, out_shape=jax.ShapeDtypeStruct((2 * NY * NZ, 4, wi...]
where the time goes in v4:
time: 49.7 us; the launch traced here: 49.5 us
  Pallas kernels  47.5 us (96%)
  local copies, waits for them, and re-layouts  2.02 us (4%)
    pallas_call x1, Pallas kernels, shards(): pl.pallas_call(kernel, out_shape=jax.ShapeDtypeStruct((2 * NY * NZ, 4, wi...  47.5 us
    unnamed x1, local copies, waits for them, and re-layouts  2.02 us

profile of v4, /device:TPU:1, one launch (start us, length us, event | category | flops | bytes accessed | tf_op | source)
XLA Modules:
  0.0 49.5 jit_solution(8388784180338371650)
XLA Ops:
  0.0 47.5 %shard_map.37 = bf16[128,4,512]{2,1,0:T(4,128)(2,1)} custom-call(bf16[16,1024]{1,0:T(8,128)(2,1)} %amp_ref.1, s32[1,16]{1,0:T(1,128)} %pat_ref.1, bf16[1024,512]{1,0:T(8,128)(2,1)} %int_ref.1), custom_call_target="tpu_custom_call" | custom-call | tf_op jit(solution)/shard_map/pallas_call | solution.py:341
  47.5 2.0 %copy.5 = bf16[128,4,512]{2,1,0:T(4,128)(2,1)} copy(bf16[128,4,512]{2,1,0:T(4,128)(2,1)} %shard_map.37) | data formatting | bytes 1048576

commit v5 on v4

--- a/solution.py
+++ b/solution.py
@@ -288,13 +288,13 @@
     from_y(3)
     send_on(1)
     unpack(2)
+    from_y(4)
     load_b.wait()
     for i in range(PARTS):
         for side in range(2):
             if i // half != side:
                 arrival(side, i).wait_recv()
     multiply(0, BATCHES[2][1], (0, 1, 3), False)
-    from_y(4)
     unpack(3)
     middle, most = BATCHES[2][1], BATCHES[-2][1]
     multiply(middle, most, (0, 1, 3), False)
@@ -332,6 +332,10 @@
             own_slice(side, i).wait_send()
         for i in range(half):
             next_slice(side, i).wait_send()
+
+
+def hand_over(from_ref, to_ref):
+    to_ref[...] = from_ref[...]
 
 
 def shards(amplitudes, integrals, pattern):
@@ -372,7 +376,12 @@
             collective_id=0, has_side_effects=True, vmem_limit_bytes=62 * 2**20
         ),
     )(amplitudes, pattern, integrals)
-    return out
+    return pl.pallas_call(
+        hand_over,
+        out_shape=jax.ShapeDtypeStruct(out.shape, out.dtype),
+        in_specs=[pl.BlockSpec(memory_space=pltpu.VMEM)],
+        out_specs=pl.BlockSpec(memory_space=pltpu.VMEM),
+    )(out)
 
 
 def solution(mesh):

time: 49.7 us -> 49.2 us (0.990)
  local copies, waits for them, and re-layouts: 2.02 us -> 0 us
  Pallas kernels: 47.5 us -> 48.9 us
    unnamed x1 -> x0, local copies, waits for them, and re-layouts: 2.02 us -> none
    pallas_call x0 -> x1, Pallas kernels: none -> 1.87 us  [shards(): pl.pallas_call(hand_over, out_shape=jax.ShapeDtypeStruct(out.shape, out.d...]
where the time goes in v5:
time: 49.2 us; the launch traced here: 48.9 us
  Pallas kernels  48.9 us (99%)
    pallas_call x1, Pallas kernels, shards(): pl.pallas_call(kernel, out_shape=jax.ShapeDtypeStruct((2 * NY * NZ, 4, wi...  47 us
    pallas_call x1, Pallas kernels, shards(): pl.pallas_call(hand_over, out_shape=jax.ShapeDtypeStruct(out.shape, out.d...  1.87 us

profile of v5, /device:TPU:1, one launch (start us, length us, event | category | flops | bytes accessed | tf_op | source)
XLA Modules:
  0.0 48.9 jit_solution(6866189049192549804)
XLA Ops:
  0.0 47.0 %shard_map.37.from_ref = bf16[128,4,512]{2,1,0:T(4,128)(2,1)} custom-call(bf16[16,1024]{1,0:T(8,128)(2,1)} %amp_ref.1, s32[1,16]{1,0:T(1,128)} %pat_ref.1, bf16[1024,512]{1,0:T(8,128)(2,1)} %int_ref.1), custom_call_target="tpu_custom_call" | custom-call | tf_op jit(solution)/shard_map/pallas_call | solution.py:345
  47.0 1.9 %shard_map.38 = bf16[128,4,512]{2,1,0:T(4,128)(2,1)} custom-call(bf16[128,4,512]{2,1,0:T(4,128)(2,1)} %shard_map.37.from_ref), custom_call_target="tpu_custom_call" | custom-call | tf_op jit(solution)/shard_map/pallas_call | solution.py:379

commit v6 on v5

--- a/solution.py
+++ b/solution.py
@@ -282,11 +282,11 @@
     from_z(3)
     from_z(4)
     send_on(0)
+    send_on(1)
     from_y(2)
     unpack(0)
     unpack(1)
     from_y(3)
-    send_on(1)
     unpack(2)
     from_y(4)
     load_b.wait()

time: 49.2 us -> 49.2 us (level)
  no operation moved by 1% of the time
where the time goes in v6:
time: 49.2 us; the launch traced here: 48.9 us
  Pallas kernels  48.9 us (99%)
    pallas_call x1, Pallas kernels, shards(): pl.pallas_call(kernel, out_shape=jax.ShapeDtypeStruct((2 * NY * NZ, 4, wi...  47 us
    pallas_call x1, Pallas kernels, shards(): pl.pallas_call(hand_over, out_shape=jax.ShapeDtypeStruct(out.shape, out.d...  1.87 us

profile of v6, /device:TPU:1, one launch (start us, length us, event | category | flops | bytes accessed | tf_op | source)
XLA Modules:
  0.0 48.9 jit_solution(6542501645209548317)
XLA Ops:
  0.0 47.0 %shard_map.37.from_ref = bf16[128,4,512]{2,1,0:T(4,128)(2,1)} custom-call(bf16[16,1024]{1,0:T(8,128)(2,1)} %amp_ref.1, s32[1,16]{1,0:T(1,128)} %pat_ref.1, bf16[1024,512]{1,0:T(8,128)(2,1)} %int_ref.1), custom_call_target="tpu_custom_call" | custom-call | tf_op jit(solution)/shard_map/pallas_call | solution.py:345
  47.0 1.9 %shard_map.38 = bf16[128,4,512]{2,1,0:T(4,128)(2,1)} custom-call(bf16[128,4,512]{2,1,0:T(4,128)(2,1)} %shard_map.37.from_ref), custom_call_target="tpu_custom_call" | custom-call | tf_op jit(solution)/shard_map/pallas_call | solution.py:379

commit v7 on v6

--- a/solution.py
+++ b/solution.py
@@ -285,8 +285,8 @@
     send_on(1)
     from_y(2)
     unpack(0)
+    from_y(3)
     unpack(1)
-    from_y(3)
     unpack(2)
     from_y(4)
     load_b.wait()

time: 49.2 us -> 50.7 us (1.030)
  Pallas kernels: 48.9 us -> 49.9 us
    pallas_call x1, Pallas kernels: 47 us -> 48.1 us  [shards(): pl.pallas_call(kernel, out_shape=jax.ShapeDtypeStruct((2 * NY * NZ, 4, wi...]
where the time goes in v7:
time: 50.7 us; the launch traced here: 50 us
  Pallas kernels  49.9 us (98%)
    pallas_call x1, Pallas kernels, shards(): pl.pallas_call(kernel, out_shape=jax.ShapeDtypeStruct((2 * NY * NZ, 4, wi...  48.1 us
    pallas_call x1, Pallas kernels, shards(): pl.pallas_call(hand_over, out_shape=jax.ShapeDtypeStruct(out.shape, out.d...  1.87 us

profile of v7, /device:TPU:1, one launch (start us, length us, event | category | flops | bytes accessed | tf_op | source)
XLA Modules:
  0.0 50.0 jit_solution(17241085293893768523)
XLA Ops:
  0.0 48.1 %shard_map.37.from_ref = bf16[128,4,512]{2,1,0:T(4,128)(2,1)} custom-call(bf16[16,1024]{1,0:T(8,128)(2,1)} %amp_ref.1, s32[1,16]{1,0:T(1,128)} %pat_ref.1, bf16[1024,512]{1,0:T(8,128)(2,1)} %int_ref.1), custom_call_target="tpu_custom_call" | custom-call | tf_op jit(solution)/shard_map/pallas_call | solution.py:345
  48.1 1.9 %shard_map.38 = bf16[128,4,512]{2,1,0:T(4,128)(2,1)} custom-call(bf16[128,4,512]{2,1,0:T(4,128)(2,1)} %shard_map.37.from_ref), custom_call_target="tpu_custom_call" | custom-call | tf_op jit(solution)/shard_map/pallas_call | solution.py:379
